TPU v7x, 128 devices: a whole 4x4x4 slice. The times are simulated.
128 devices in a mesh: zg: 4 (over x), ma: 32 (over y, z, core).
Axes of the slice: x: 4, y: 4, z: 4, core: 2. Of those that a mesh axis runs over, the one named last changes fastest.
Arguments:
- forward_coef: bfloat16 [512, 128, 2, 2, 512], P('ma', 'zg'), may hold values from -6 to 6
- adjoint_coef: bfloat16 [512, 128, 2, 2, 512], P('ma', 'zg'), may hold values from -6 to 6
- radial_table: bfloat16 [512, 512, 512], P('ma'), may hold values from -0.25 to 0.25
- radial_count: int32 [512], replicated, may hold values from 1 to 512, as said below
- mode_blocks: int32 [32], replicated, may hold values from 0 to 31, each once
Outputs:
- adjoint_rhs: bfloat16 [512, 128, 2, 2, 512], P('ma', 'zg')
Inputs may be any that keep to these rules, and one draw needn't show every extreme that they name: radial_count[m] counts the live radial degrees of azimuthal mode m under a triangular truncation. Each block number appears once; slot block b holds the azimuthal modes mode_blocks[b] * 16 to mode_blocks[b] * 16 + 15.
All inputs are finite; a program needn't handle non-finite values.
Results may differ from a plain program's by a relative error of at most 0.015.
Values may be sent and summed in bfloat16 or wider, within the bound.
A program may use at most 128 MiB of HBM per device.

v0:
```python
import functools
import math

import jax
import jax.numpy as jnp
import numpy as np
from jax import lax
from jax.experimental import pallas as pl
from jax.experimental.pallas import tpu as pltpu
from jax.sharding import PartitionSpec as P

M = 512
NN = 512
K = 128
NPHI = 1024
MA_DIMS = (4, 4, 2)
MESH = pl.DeviceIdType.MESH
BF16 = jnp.bfloat16
F32 = jnp.float32


def constant_tables():
    index = np.arange(M, dtype=np.int64)[:, None] * np.arange(NPHI, dtype=np.int64)[None, :] % NPHI
    angles = index.astype(np.float64) * (2.0 * math.pi / NPHI)
    fourier = np.concatenate([np.cos(angles), np.sin(angles)]) * math.sqrt(2.0 / NPHI)
    degree = np.arange(K, dtype=np.int64)
    cheb_index = degree[:, None] * (2 * degree[None, :] + 1) % (4 * K)
    cheb = np.cos(cheb_index.astype(np.float64) * (math.pi / (2 * K))) * math.sqrt(2.0 / K)
    fourier = fourier.astype(np.float32).astype(BF16)
    cheb = cheb.astype(np.float32).astype(BF16)
    return fourier, np.ascontiguousarray(fourier.T), cheb, np.ascontiguousarray(cheb.T)


def kernel(dims, rad0, rad1, fourier_hbm, fourier_t_hbm, cheb_ref, cheb_t_ref, mode_row, mode_col, out_ref,
           recv_x, send_y, recv_y, plane, table, table_t, raw, raw_t, grid0, source, send_b, recv_b, send_bx,
           load_sem, local_x, local_y, local_b, local_o, ssem_x, ssem_y, ssem_b, ssem_o, sem_x, sem_y, sem_b, sem_o):
    nx, ma_dims, slots, kd, zd = dims
    ny, nz, nc = ma_dims
    ma = ny * nz * nc
    kk = nx * kd
    x = lax.axis_index("zg")
    m = lax.axis_index("ma")
    my, mz, mc = m // (nz * nc), (m // nc) % nz, m % nc

    def ma_peer(j):
        dy, dz, dc = j // (nz * nc), (j // nc) % nz, j % nc
        return ((my + dy) % ny) * (nz * nc) + ((mz + dz) % nz) * nc + (mc + dc) % nc

    def x_peer(j):
        return (x + j) % nx

    loads = [
        pltpu.make_async_copy(fourier_t_hbm, raw_t, load_sem.at[0]),
        pltpu.make_async_copy(fourier_hbm, raw, load_sem.at[1]),
    ]
    for load in loads:
        load.start()

    barrier = pltpu.get_barrier_semaphore()

    def signal_ma(j, carry):
        pl.semaphore_signal(barrier, inc=1, device_id=(x, ma_peer(j)), device_id_type=MESH)
        return carry

    lax.fori_loop(1, ma, signal_ma, 0)
    for j in range(1, nx):
        pl.semaphore_signal(barrier, inc=1, device_id=(x_peer(j), m), device_id_type=MESH)
    pl.semaphore_wait(barrier, ma - 1 + nx - 1)

    def lane(j):
        return pl.ds(pl.multiple_of(j * 128, 128), 128)

    for ch in range(8):
        field, part = ch // 2, ch % 2
        rad = (rad0, rad1)[field // 2]
        for j in (1, nx - 1) + tuple(range(2, nx - 1)) if nx > 2 else (1,):
            pltpu.make_async_remote_copy(
                src_ref=rad.at[:, part, field % 2, :, lane(x_peer(j))],
                dst_ref=recv_x.at[ch, x],
                send_sem=ssem_x,
                recv_sem=sem_x.at[ch],
                device_id=(x_peer(j), m),
                device_id_type=MESH,
            ).start()
        pltpu.make_async_copy(rad.at[:, part, field % 2, :, lane(x)], recv_x.at[ch, x], local_x.at[ch]).start()

    modes = M
    for load in loads:
        load.wait()
    one_hot = (lax.broadcasted_iota(jnp.int32, (modes, modes), 0) == mode_row[...]).astype(F32).astype(BF16)
    one_hot_t = (lax.broadcasted_iota(jnp.int32, (modes, modes), 1) == mode_col[...]).astype(F32).astype(BF16)
    for part in range(2):
        half = pl.ds(part * modes, modes)
        table_t[:, half] = jnp.dot(raw_t[:, half], one_hot, preferred_element_type=F32).astype(BF16)
        table[half, :] = jnp.dot(one_hot_t, raw[half, :], preferred_element_type=F32).astype(BF16)

    def cheb_chunk(ch, carry):
        pltpu.make_async_copy(recv_x.at[ch, x], recv_x.at[ch, x], local_x.at[ch]).wait()
        pltpu.make_async_remote_copy(
            src_ref=recv_x.at[ch, pl.ds(0, nx - 1)], dst_ref=recv_x.at[ch, pl.ds(0, nx - 1)],
            send_sem=ssem_x, recv_sem=sem_x.at[ch], device_id=(x_peer(1), m), device_id_type=MESH,
        ).wait_recv()
        for s in range(0, slots, 2):
            pair = jnp.concatenate([recv_x[ch, :, s + i].reshape(kk, 128) for i in range(2)], axis=1)
            levels = jnp.dot(cheb_t_ref[...], pair, preferred_element_type=F32)
            for i in range(2):
                plane[pl.ds(s + i, kk, stride=slots), :] = levels[:, 128 * i:128 * (i + 1)]
        send_y[ch] = plane[...].astype(BF16).reshape(ma, zd, slots, 128)

        def send(j, carry):
            peer = ma_peer(j)
            pltpu.make_async_remote_copy(
                src_ref=send_y.at[ch, peer], dst_ref=recv_y.at[ch, m],
                send_sem=ssem_y, recv_sem=sem_y.at[ch], device_id=(x, peer), device_id_type=MESH,
            ).start()
            return carry

        lax.fori_loop(1, ma, send, 0)
        pltpu.make_async_copy(send_y.at[ch, m], recv_y.at[ch, m], local_y.at[ch]).start()
        return carry

    def wait_y(ch, carry):
        pltpu.make_async_copy(recv_y.at[ch, m], recv_y.at[ch, m], local_y.at[ch]).wait()
        pltpu.make_async_remote_copy(
            src_ref=recv_y.at[ch, pl.ds(0, ma - 1)], dst_ref=recv_y.at[ch, pl.ds(0, ma - 1)],
            send_sem=ssem_y, recv_sem=sem_y.at[ch], device_id=(x, ma_peer(1)), device_id_type=MESH,
        ).wait_recv()
        return carry

    def levels_of(arg, z):
        columns = []
        for f2 in range(2):
            first = (arg * 2 + f2) * 2
            columns.append(jnp.concatenate(
                [recv_y[first + part, :, z].reshape(modes, 128) for part in range(2)], axis=0))
        return jnp.concatenate(columns, axis=1)

    lax.fori_loop(0, 5, cheb_chunk, 0)
    lax.fori_loop(0, 4, wait_y, 0)

    def forward_grid(z, carry):
        grid0[z] = jnp.dot(table_t[...], levels_of(0, z), preferred_element_type=F32)
        return carry

    lax.fori_loop(0, zd, forward_grid, 0)
    lax.fori_loop(5, 8, cheb_chunk, 0)
    lax.fori_loop(4, 8, wait_y, 0)

    def back_send(ch, z, count):
        def send(j, carry):
            peer = ma_peer(j)
            pltpu.make_async_remote_copy(
                src_ref=send_b.at[ch, peer, pl.ds(z, count)], dst_ref=recv_b.at[ch, m, pl.ds(z, count)],
                send_sem=ssem_b, recv_sem=sem_b.at[ch], device_id=(x, peer), device_id_type=MESH,
            ).start()
            return carry

        lax.fori_loop(1, ma, send, 0)

    def products(z, carry):
        adjoint = jnp.dot(table_t[...], levels_of(1, z), preferred_element_type=F32)
        velocity, heat = grid0[z, :, :128], grid0[z, :, 128:]
        velocity_adj, heat_adj = adjoint[:, :128], adjoint[:, 128:]
        source[:, :128] = (velocity * velocity_adj + heat * heat_adj).astype(BF16)
        source[:, 128:] = (velocity * heat_adj - heat * velocity_adj).astype(BF16)
        back = jnp.dot(table[...], source[...], preferred_element_type=F32).astype(BF16)
        for g in range(2):
            for part in range(2):
                send_b[g * 2 + part, :, z] = back[part * modes:(part + 1) * modes,
                                                  128 * g:128 * (g + 1)].reshape(ma, slots, 128)
        back_send(0, z, 1)
        return carry

    lax.fori_loop(0, zd, products, 0)
    for ch in range(1, 4):
        back_send(ch, 0, zd)
    for ch in range(4):
        pltpu.make_async_copy(send_b.at[ch, m], recv_b.at[ch, m], local_b.at[ch]).start()

    for ch in range(4):
        g, part = ch // 2, ch % 2
        pltpu.make_async_copy(recv_b.at[ch, m], recv_b.at[ch, m], local_b.at[ch]).wait()
        pltpu.make_async_remote_copy(
            src_ref=recv_b.at[ch, pl.ds(0, ma - 1)], dst_ref=recv_b.at[ch, pl.ds(0, ma - 1)],
            send_sem=ssem_b, recv_sem=sem_b.at[ch], device_id=(x, ma_peer(1)), device_id_type=MESH,
        ).wait_recv()
        plane[...] = recv_b[ch].reshape(kk * slots, 128).astype(F32)
        for s in range(0, slots, 2):
            pair = jnp.concatenate([plane[pl.ds(s + i, kk, stride=slots), :] for i in range(2)], axis=1).astype(BF16)
            degrees = jnp.dot(cheb_ref[...], pair, preferred_element_type=F32).astype(BF16)
            for i in range(2):
                send_bx[ch, :, s + i] = degrees[:, 128 * i:128 * (i + 1)].reshape(nx, kd, 128)
        for j in (1, nx - 1) + tuple(range(2, nx - 1)) if nx > 2 else (1,):
            pltpu.make_async_remote_copy(
                src_ref=send_bx.at[ch, x_peer(j)], dst_ref=out_ref.at[:, part, g, :, lane(x)],
                send_sem=ssem_o, recv_sem=sem_o.at[ch], device_id=(x_peer(j), m), device_id_type=MESH,
            ).start()
        pltpu.make_async_copy(send_bx.at[ch, x], out_ref.at[:, part, g, :, lane(x)], local_o.at[ch]).start()

    for ch in range(4):
        g, part = ch // 2, ch % 2
        pltpu.make_async_copy(send_bx.at[ch, x], out_ref.at[:, part, g, :, lane(x)], local_o.at[ch]).wait()
        pltpu.make_async_remote_copy(
            src_ref=send_bx.at[ch, pl.ds(0, nx - 1)], dst_ref=send_bx.at[ch, pl.ds(0, nx - 1)],
            send_sem=ssem_o, recv_sem=sem_o.at[ch], device_id=(x_peer(1), m), device_id_type=MESH,
        ).wait()
    for buffer, count, sem in ((recv_x, nx - 1, ssem_x), (recv_y, ma - 1, ssem_y), (recv_b, ma - 1, ssem_b)):
        part_ref = buffer.at[:, pl.ds(0, count)]
        pltpu.make_async_remote_copy(
            src_ref=part_ref, dst_ref=part_ref, send_sem=sem, recv_sem=sem,
            device_id=(x_peer(1), m), device_id_type=MESH,
        ).wait_send()


def middle(ma_dims, rad0, rad1, mode_of_slot):
    nx = lax.axis_size("zg")
    ma = lax.axis_size("ma")
    slots, _, _, kd, _ = rad0.shape
    kk = nx * kd
    zd = kk // ma
    fourier, fourier_t, cheb, cheb_t = constant_tables()
    any_spec = pl.BlockSpec(memory_space=pl.ANY)
    vmem_spec = pl.BlockSpec(memory_space=pltpu.VMEM)
    dma = pltpu.SemaphoreType.DMA
    return pl.pallas_call(
        functools.partial(kernel, (nx, ma_dims, slots, kd, zd)),
        out_shape=jax.ShapeDtypeStruct((slots, 2, 2, kd, nx * 128), BF16),
        in_specs=[any_spec] * 4 + [vmem_spec] * 4,
        out_specs=any_spec,
        scratch_shapes=[
            pltpu.VMEM((8, nx, slots, kd, 128), BF16),
            pltpu.VMEM((8, ma, zd, slots, 128), BF16),
            pltpu.VMEM((8, ma, zd, slots, 128), BF16),
            pltpu.VMEM((kk * slots, 128), F32),
            pltpu.VMEM((2 * M, NPHI), BF16),
            pltpu.VMEM((NPHI, 2 * M), BF16),
            pltpu.VMEM((2 * M, NPHI), BF16),
            pltpu.VMEM((NPHI, 2 * M), BF16),
            pltpu.VMEM((zd, NPHI, 256), F32),
            pltpu.VMEM((NPHI, 256), BF16),
            pltpu.VMEM((4, ma, zd, slots, 128), BF16),
            pltpu.VMEM((4, ma, zd, slots, 128), BF16),
            pltpu.VMEM((4, nx, slots, kd, 128), BF16),
            dma((2,)), dma((8,)), dma((8,)), dma((4,)), dma((4,)),
            dma, dma, dma, dma,
            dma((8,)), dma((8,)), dma((4,)), dma((4,)),
        ],
        compiler_params=pltpu.CompilerParams(
            collective_id=1, has_side_effects=True, vmem_limit_bytes=56 * 2**20
        ),
    )(rad0, rad1, jnp.asarray(fourier), jnp.asarray(fourier_t), jnp.asarray(cheb), jnp.asarray(cheb_t),
      mode_of_slot.reshape(1, M), mode_of_slot.reshape(M, 1))


def body(ma_dims, forward_coef, adjoint_coef, radial_table, radial_count, mode_blocks):
    slots = forward_coef.shape[0]
    group = jnp.arange(lax.axis_size("ma"), dtype=jnp.int32)
    own_block = jnp.sum(jnp.where(group == lax.axis_index("ma"), mode_blocks, 0))
    slot_index = jnp.arange(slots, dtype=jnp.int32)
    own_modes = own_block * slots + slot_index
    mode_of_slot = (mode_blocks[:, None] * slots + slot_index[None, :]).reshape(M)
    mode_index = jnp.arange(M, dtype=jnp.int32)
    live_count = jnp.sum(jnp.where(own_modes[:, None] == mode_index[None, :], radial_count[None, :], 0), axis=1)
    live = jnp.arange(NN, dtype=jnp.int32)[None, :] < live_count[:, None]
    masked_table = jnp.where(live[:, :, None], radial_table, jnp.zeros((), BF16))
    radial = [
        jnp.einsum("skcfn,snr->scfkr", coef, masked_table, preferred_element_type=F32).astype(BF16)
        for coef in (forward_coef, adjoint_coef)
    ]
    back = middle(ma_dims, radial[0], radial[1], mode_of_slot)
    return jnp.einsum("scgkr,snr->skcgn", back, masked_table, preferred_element_type=F32).astype(BF16)


def solution(mesh):
    placed = (P("ma", "zg", None, None, None), P("ma", "zg", None, None, None), P("ma", None, None), P(), P())
    return jax.shard_map(
        functools.partial(body, MA_DIMS), mesh=mesh, in_specs=placed,
        out_specs=P("ma", "zg", None, None, None), check_vma=False,
    )
```

profile of v0, /device:TPU:0, one launch (start us, length us, event | category | flops | bytes accessed | tf_op | source)
XLA Modules:
  0.0 137.3 jit_solution(9457952019945094829)
XLA Ops:
  0.0 0.0 copy-start
  0.0 1.4 %broadcast_multiply_fusion = (s32[32]{0:T(128)S(1)}, s32[]{:T(128)}) fusion(s32[32]{0:T(128)} %param.13, s32[]{:T(128)S(6)} %axis_index.12), kind=kLoop, calls=%fused_computation.22 | loop fusion | flops 127 | bytes 264 | tf_op jit(solution)/shard_map/mul | solution.py:261
  2.1 0.9 select_reduce_fusion
  3.0 0.1 iota_compare_fusion.1
  3.1 0.1 iota_add_fusion
  3.1 0.7 add.48.mode_row
  3.8 0.8 add.50.mode_col
  4.7 0.0 copy-done
  4.7 0.0 copy-start.1
  4.7 0.0 copy-start.2
  4.7 6.0 %convert_bitcast_fusion.1.rad1 = bf16[16,2,2,32,512]{4,3,2,1,0:T(8,128)(2,1)} fusion(bf16[16,32,2,2,512]{4,3,2,1,0:T(2,128)(2,1)S(1)} %copy-done, bf16[16,512,512]{2,1,0:T(8,128)(2,1)} %param.11, pred[16,512]{1,0:T(8,128)(4,1)S(1)} %iota_compare_fusion.1), kind=kOutput, calls=%fused_computation.13 | convolution fusion | flops 1078984704 | bytes 12591104 | tf_op jit(solution)/shard_map/skcfn,snr->scfkr/dot_general | solution.py:267
  10.6 0.6 copy-done.1
  11.2 0.6 copy-done.2
  11.8 3.3 %convert_bitcast_fusion.2.rad0 = bf16[16,2,2,32,512]{4,3,2,1,0:T(8,128)(2,1)} fusion(bf16[16,32,2,2,512]{4,3,2,1,0:T(2,128)(2,1)S(1)} %copy-done.2, bf16[16,512,512]{2,1,0:T(8,128)(2,1)S(1)} %copy-done.1, pred[16,512]{1,0:T(8,128)(4,1)S(1)} %iota_compare_fusion.1), kind=kOutput, calls=%fused_computation.14 | convolution fusion | flops 1078984704 | bytes 12591104 | tf_op jit(solution)/shard_map/skcfn,snr->scfkr/dot_general | solution.py:267
  15.1 113.0 %shard_map.91 = bf16[16,2,2,32,512]{4,3,2,1,0:T(8,128)(2,1)} custom-call(bf16[16,2,2,32,512]{4,3,2,1,0:T(8,128)(2,1)} %convert_bitcast_fusion.2.rad0, bf16[16,2,2,32,512]{4,3,2,1,0:T(8,128)(2,1)} %convert_bitcast_fusion.1.rad1, bf16[1024,1024]{1,0:T(8,128)(2,1)} %constant.7.clone.fourier_hbm, bf16[1024,1024]{1,0:T(8,128)(2,1)} %constant.20.clone.fourier_t_hbm, ...), custom_call_target="tpu_custom_call" | custom-call | tf_op jit(solution)/shard_map/pallas_call | solution.py:225
  128.1 5.7 %convert_bitcast_fusion = bf16[16,32,2,2,512]{4,1,3,2,0:T(8,128)(2,1)S(1)} fusion(bf16[16,2,2,32,512]{4,3,2,1,0:T(8,128)(2,1)} %shard_map.91, bf16[16,512,512]{2,1,0:T(8,128)(2,1)} %param.11, pred[16,512]{1,0:T(8,128)(4,1)S(1)} %iota_compare_fusion.1), kind=kOutput, calls=%fused_computation.12 | convolution fusion | flops 1078984704 | bytes 12591104 | tf_op jit(solution)/shard_map/scgkr,snr->skcgn/dot_general | solution.py:271
  133.8 3.5 %copy.16 = bf16[16,32,2,2,512]{4,3,2,1,0:T(2,128)(2,1)} copy(bf16[16,32,2,2,512]{4,1,3,2,0:T(8,128)(2,1)S(1)} %convert_bitcast_fusion) | data formatting | bytes 4194304 | tf_op jit(solution)/shard_map/convert_element_type | solution.py:271
  (1 shorter events, 0.0 us)
Async XLA Ops:
  0.0 4.7 %copy-start = (bf16[16,32,2,2,512]{4,3,2,1,0:T(2,128)(2,1)S(1)}, bf16[16,32,2,2,512]{4,3,2,1,0:T(2,128)(2,1)}, u32[]{:S(2)}) copy-start(bf16[16,32,2,2,512]{4,3,2,1,0:T(2,128)(2,1)} %param.10) | copy-start | bytes 6291460
  4.7 6.6 %copy-start.1 = (bf16[16,512,512]{2,1,0:T(8,128)(2,1)S(1)}, bf16[16,512,512]{2,1,0:T(8,128)(2,1)}, u32[]{:S(2)}) copy-start(bf16[16,512,512]{2,1,0:T(8,128)(2,1)} %param.11) | copy-start | bytes 25165828
  4.7 7.2 %copy-start.2 = (bf16[16,32,2,2,512]{4,3,2,1,0:T(2,128)(2,1)S(1)}, bf16[16,32,2,2,512]{4,3,2,1,0:T(2,128)(2,1)}, u32[]{:S(2)}) copy-start(bf16[16,32,2,2,512]{4,3,2,1,0:T(2,128)(2,1)} %param.9) | copy-start | bytes 6291460
where the time goes:
time: 139 us; the launch traced here: 137 us
  Pallas kernels  113 us (81%)
  matrix products  14.9 us (11%)
  local copies, waits for them, and re-layouts  6.24 us (4%)
  other arithmetic  2.46 us (2%)
    pallas_call x1, Pallas kernels, middle(): pl.pallas_call(functools.partial(kernel, (nx, ma_dims, slots, kd, zd)), o...  113 us
    dot_general x2, matrix products, body(): jnp.einsum('skcfn,snr->scfkr', coef, masked_table, preferred_element_type...  9.21 us
    dot_general x1, matrix products, body(): jnp.einsum('scgkr,snr->skcgn', back, masked_table, preferred_element_type...  5.68 us
    convert_element_type x1, local copies, waits for them, and re-layouts, body(): jnp.einsum('scgkr,snr->skcgn', back, masked_table, preferred_element_type...  3.49 us

commit v1 on v0

v1 whole, which is shorter than its diff:
```python
import functools
import math

import jax
import jax.numpy as jnp
import numpy as np
from jax import lax
from jax.experimental import pallas as pl
from jax.experimental.pallas import tpu as pltpu
from jax.sharding import PartitionSpec as P

M = 512
NN = 512
K = 128
NPHI = 1024
MA_DIMS = (4, 4, 2)
MESH = pl.DeviceIdType.MESH
BF16 = jnp.bfloat16
F32 = jnp.float32


def constant_tables():
    index = np.arange(M, dtype=np.int64)[:, None] * np.arange(NPHI, dtype=np.int64)[None, :] % NPHI
    angles = index.astype(np.float64) * (2.0 * math.pi / NPHI)
    fourier = np.concatenate([np.cos(angles), np.sin(angles)]) * math.sqrt(2.0 / NPHI)
    degree = np.arange(K, dtype=np.int64)
    cheb_index = degree[:, None] * (2 * degree[None, :] + 1) % (4 * K)
    cheb = np.cos(cheb_index.astype(np.float64) * (math.pi / (2 * K))) * math.sqrt(2.0 / K)
    fourier = fourier.astype(np.float32).astype(BF16)
    cheb = cheb.astype(np.float32).astype(BF16)
    return fourier, np.ascontiguousarray(fourier.T), cheb, np.ascontiguousarray(cheb.T)


def kernel(dims, coef0, coef1, radial_hbm, fourier_hbm, fourier_t_hbm, cheb_ref, cheb_t_ref, count_ref, block_ref,
           out_ref, coef, radial, wide, send_x, recv_x, send_y, recv_y, plane, one_hot, raw, raw_t, table, table_t,
           source, send_b, recv_b, send_o, recv_o, wide_out, out_v,
           coef_sem, radial_sem, load_sem, out_sem, local_x, local_y, local_b, local_o,
           ssem_x, ssem_y, ssem_b, ssem_o, sem_x, sem_y, sem_b, sem_o):
    nx, ma_dims, slots, kd, zd, nbs = dims
    ny, nz, nc = ma_dims
    ma = ny * nz * nc
    kk = nx * kd
    modes = ma * slots
    row_step = 4 * nbs
    x = lax.axis_index("zg")
    m = lax.axis_index("ma")
    my, mz, mc = m // (nz * nc), (m // nc) % nz, m % nc
    x_order = (1,) if nx == 2 else (1, nx - 1) + tuple(range(2, nx - 1))

    def ma_peer(j):
        dy, dz, dc = j // (nz * nc), (j // nc) % nz, j % nc
        return ((my + dy) % ny) * (nz * nc) + ((mz + dz) % nz) * nc + (mc + dc) % nc

    def x_peer(j):
        return (x + j) % nx

    def remote(src, dst, send_sem, recv_sem, to_x, to_m):
        return pltpu.make_async_remote_copy(
            src_ref=src, dst_ref=dst, send_sem=send_sem, recv_sem=recv_sem,
            device_id=(to_x, to_m), device_id_type=MESH,
        )

    def wait_received(buffer, ch, count, sem, local_sem):
        own = buffer.at[ch, 0]
        pltpu.make_async_copy(own, own, local_sem.at[ch]).wait()
        others = buffer.at[ch, pl.ds(0, count)]
        remote(others, others, sem.at[ch], sem.at[ch], x_peer(1), m).wait_recv()

    barrier = pltpu.get_barrier_semaphore()

    def signal_ma(j, carry):
        pl.semaphore_signal(barrier, inc=1, device_id=(x, ma_peer(j)), device_id_type=MESH)
        return carry

    lax.fori_loop(1, ma, signal_ma, 0)
    for j in range(1, nx):
        pl.semaphore_signal(barrier, inc=1, device_id=(x_peer(j), m), device_id_type=MESH)

    def coef_load(arg, s):
        return pltpu.make_async_copy((coef0, coef1)[arg].at[s], coef.at[arg, s], coef_sem.at[arg, s])

    def radial_load(s):
        return pltpu.make_async_copy(radial_hbm.at[s], radial.at[s], radial_sem.at[s])

    def start_first(s, carry):
        coef_load(0, s).start()
        radial_load(s).start()
        return carry

    def start_second(s, carry):
        coef_load(1, s).start()
        return carry

    lax.fori_loop(0, slots, start_first, 0)
    lax.fori_loop(0, slots, start_second, 0)
    loads = [
        pltpu.make_async_copy(fourier_t_hbm, raw_t, load_sem.at[0]),
        pltpu.make_async_copy(fourier_hbm, raw, load_sem.at[1]),
    ]
    for load in loads:
        load.start()

    own_block = block_ref[m]
    lanes = lax.broadcasted_iota(jnp.int32, (1, 128), 1)
    low = lanes < 64

    def radial_slot(arg, s):
        coef_load(arg, s).wait()
        if arg == 0:
            radial_load(s).wait()
        live = count_ref[own_block * slots + s]
        wide[...] = coef[arg, s].astype(F32)
        rows = []
        for f in range(2):
            for part in range(2):
                tiles = []
                for nb in range(nbs):
                    tile = wide[pl.ds((part * nbs + nb) * 2 + f, kd, stride=row_step), :]
                    tiles.append(jnp.where(lanes + nb * 128 < live, tile, 0.0).astype(BF16))
                rows.append(jnp.concatenate(tiles, axis=1))
        values = jnp.dot(jnp.concatenate(rows, axis=0), radial[s], preferred_element_type=F32)
        for to in range(nx):
            first = values[:2 * kd, 128 * to:128 * (to + 1)]
            second = pltpu.roll(values[2 * kd:, 128 * to:128 * (to + 1)], 64, 1)
            halves = (jnp.where(low, first, second).astype(BF16), jnp.where(low, second, first).astype(BF16))
            for h in range(2):
                for part in range(2):
                    send_x[h * 4 + arg * 2 + part, to, s] = halves[h][part * kd:(part + 1) * kd]

    def x_send(ch):
        for j in x_order:
            remote(send_x.at[ch, x_peer(j)], recv_x.at[ch, x], ssem_x, sem_x.at[ch], x_peer(j), m).start()
        pltpu.make_async_copy(send_x.at[ch, x], recv_x.at[ch, x], local_x.at[ch]).start()

    def radial_first(s, carry):
        radial_slot(0, s)
        return carry

    def radial_second(s, carry):
        radial_slot(1, s)
        return carry

    lax.fori_loop(0, slots, radial_first, 0)
    pl.semaphore_wait(barrier, ma - 1 + nx - 1)
    for ch in (0, 1):
        x_send(ch)
    lax.fori_loop(0, slots, radial_second, 0)
    for ch in (2, 3, 4, 5, 6, 7):
        x_send(ch)

    def one_hot_block(j, carry):
        start = pl.multiple_of(j * slots, slots)
        column = lax.broadcasted_iota(jnp.int32, (slots, modes), 1)
        row = lax.broadcasted_iota(jnp.int32, (slots, modes), 0)
        one_hot[pl.ds(start, slots), :] = (column == row + block_ref[j] * slots).astype(F32).astype(BF16)
        return carry

    lax.fori_loop(0, ma, one_hot_block, 0)
    for load in loads:
        load.wait()
    for part in range(2):
        half = pl.ds(part * modes, modes)
        table_t[:, half] = lax.dot_general(
            raw_t[:, half], one_hot[...], (((1,), (1,)), ((), ())), preferred_element_type=F32).astype(BF16)
        table[half, :] = jnp.dot(one_hot[...], raw[half, :], preferred_element_type=F32).astype(BF16)

    def cheb_chunk(ch, carry):
        wait_received(recv_x, ch, nx - 1, sem_x, local_x)
        for s in range(0, slots, 2):
            pair = jnp.concatenate([recv_x[ch, :, s + i].reshape(kk, 128) for i in range(2)], axis=1)
            levels = jnp.dot(cheb_t_ref[...], pair, preferred_element_type=F32)
            for i in range(2):
                plane[pl.ds(s + i, kk, stride=slots), :] = levels[:, 128 * i:128 * (i + 1)]
        send_y[ch] = plane[...].astype(BF16).reshape(ma, zd, slots, 128)

        def send(j, carry):
            peer = ma_peer(j)
            remote(send_y.at[ch, peer], recv_y.at[ch, m], ssem_y, sem_y.at[ch], x, peer).start()
            return carry

        lax.fori_loop(1, ma, send, 0)
        pltpu.make_async_copy(send_y.at[ch, m], recv_y.at[ch, m], local_y.at[ch]).start()
        return carry

    def wait_y(ch, carry):
        wait_received(recv_y, ch, ma - 1, sem_y, local_y)
        return carry

    def products(h, z):
        columns = []
        for i in range(2):
            for arg in range(2):
                columns.append(jnp.concatenate(
                    [recv_y[h * 4 + arg * 2 + part, :, z + i].reshape(modes, 128) for part in range(2)], axis=0))
        grid = jnp.dot(table_t[...], jnp.concatenate(columns, axis=1), preferred_element_type=F32)
        for i in range(2):
            forward = grid[:, 256 * i:256 * i + 128]
            adjoint = grid[:, 256 * i + 128:256 * i + 256]
            straight = forward * adjoint
            crossed = forward * pltpu.roll(adjoint, 64, 1)
            first = straight + pltpu.roll(straight, 64, 1)
            second = pltpu.roll(crossed, 64, 1) - crossed
            pick = (first, second) if h == 0 else (second, first)
            source[:, 128 * i:128 * (i + 1)] = jnp.where(low, pick[0], pick[1]).astype(BF16)
        back = jnp.dot(table[...], source[...], preferred_element_type=F32).astype(BF16)
        for i in range(2):
            for part in range(2):
                send_b[h * 2 + part, :, z + i] = back[part * modes:(part + 1) * modes,
                                                      128 * i:128 * (i + 1)].reshape(ma, slots, 128)

    def back_send(ch):
        def send(j, carry):
            peer = ma_peer(j)
            remote(send_b.at[ch, peer], recv_b.at[ch, m], ssem_b, sem_b.at[ch], x, peer).start()
            return carry

        lax.fori_loop(1, ma, send, 0)
        pltpu.make_async_copy(send_b.at[ch, m], recv_b.at[ch, m], local_b.at[ch]).start()

    lax.fori_loop(0, 5, cheb_chunk, 0)
    lax.fori_loop(0, 4, wait_y, 0)
    for step in range(zd // 2):
        products(0, 2 * step)
        if step == 0:
            lax.fori_loop(5, 6, cheb_chunk, 0)
    lax.fori_loop(6, 8, cheb_chunk, 0)
    for ch in (0, 1):
        back_send(ch)
    lax.fori_loop(4, 8, wait_y, 0)
    for step in range(zd // 2):
        products(1, 2 * step)
    for ch in (2, 3):
        back_send(ch)

    def cheb_back(ch, carry):
        wait_received(recv_b, ch, ma - 1, sem_b, local_b)
        plane[...] = recv_b[ch].reshape(kk * slots, 128).astype(F32)
        for s in range(0, slots, 2):
            pair = jnp.concatenate([plane[pl.ds(s + i, kk, stride=slots), :] for i in range(2)], axis=1).astype(BF16)
            degrees = jnp.dot(cheb_ref[...], pair, preferred_element_type=F32).astype(BF16)
            for i in range(2):
                send_o[ch, :, s + i] = degrees[:, 128 * i:128 * (i + 1)].reshape(nx, kd, 128)
        for j in x_order:
            remote(send_o.at[ch, x_peer(j)], recv_o.at[ch, x], ssem_o, sem_o.at[ch], x_peer(j), m).start()
        pltpu.make_async_copy(send_o.at[ch, x], recv_o.at[ch, x], local_o.at[ch]).start()
        return carry

    lax.fori_loop(0, 4, cheb_back, 0)

    def out_copy(s):
        return pltpu.make_async_copy(out_v.at[s], out_ref.at[s], out_sem.at[s])

    def radial_back(part, s):
        live = count_ref[own_block * slots + s]
        first, second = [], []
        for at in range(nx):
            near = recv_o[part, at, s].astype(F32)
            far = recv_o[2 + part, at, s].astype(F32)
            first.append(jnp.where(low, near, far).astype(BF16))
            second.append(pltpu.roll(jnp.where(low, far, near), 64, 1).astype(BF16))
        rows = jnp.concatenate([jnp.concatenate(first, axis=1), jnp.concatenate(second, axis=1)], axis=0)
        values = lax.dot_general(rows, radial[s], (((1,), (1,)), ((), ())), preferred_element_type=F32)
        for g in range(2):
            for nb in range(nbs):
                tile = values[g * kd:(g + 1) * kd, 128 * nb:128 * (nb + 1)]
                wide_out[s, pl.ds((part * nbs + nb) * 2 + g, kd, stride=row_step), :] = jnp.where(
                    lanes + nb * 128 < live, tile, 0.0)
        if part == 1:
            out_v[s] = wide_out[s].astype(BF16)
            out_copy(s).start()

    def radial_back_first(s, carry):
        radial_back(0, s)
        return carry

    def radial_back_second(s, carry):
        radial_back(1, s)
        return carry

    for ch in (0, 2):
        wait_received(recv_o, ch, nx - 1, sem_o, local_o)
    lax.fori_loop(0, slots, radial_back_first, 0)
    for ch in (1, 3):
        wait_received(recv_o, ch, nx - 1, sem_o, local_o)
    lax.fori_loop(0, slots, radial_back_second, 0)

    def finish(s, carry):
        out_copy(s).wait()
        return carry

    lax.fori_loop(0, slots, finish, 0)
    for buffer, count, sem in (
        (recv_x, nx - 1, ssem_x), (recv_y, ma - 1, ssem_y), (recv_b, ma - 1, ssem_b), (recv_o, nx - 1, ssem_o)
    ):
        sent = buffer.at[:, pl.ds(0, count)]
        remote(sent, sent, sem, sem, x_peer(1), m).wait_send()


def body(ma_dims, forward_coef, adjoint_coef, radial_table, radial_count, mode_blocks):
    nx = lax.axis_size("zg")
    ma = lax.axis_size("ma")
    slots, kd = forward_coef.shape[:2]
    kk = nx * kd
    zd = kk // ma
    nbs = NN // 128
    coef_rows = kd * 2 * nbs * 2

    def to_rows(array):
        blocks = array.reshape(slots, kd * 2, 2, nbs, 128).transpose(0, 1, 3, 2, 4)
        return blocks.reshape(slots, coef_rows, 128)

    fourier, fourier_t, cheb, cheb_t = constant_tables()
    any_spec = pl.BlockSpec(memory_space=pl.ANY)
    vmem_spec = pl.BlockSpec(memory_space=pltpu.VMEM)
    smem_spec = pl.BlockSpec(memory_space=pltpu.SMEM)
    dma = pltpu.SemaphoreType.DMA
    rows = pl.pallas_call(
        functools.partial(kernel, (nx, ma_dims, slots, kd, zd, nbs)),
        out_shape=jax.ShapeDtypeStruct((slots, coef_rows, 128), BF16),
        in_specs=[any_spec] * 5 + [vmem_spec] * 2 + [smem_spec] * 2,
        out_specs=any_spec,
        scratch_shapes=[
            pltpu.VMEM((2, slots, coef_rows, 128), BF16),
            pltpu.VMEM(radial_table.shape, BF16),
            pltpu.VMEM((coef_rows, 128), F32),
            pltpu.VMEM((8, nx, slots, kd, 128), BF16),
            pltpu.VMEM((8, nx, slots, kd, 128), BF16),
            pltpu.VMEM((8, ma, zd, slots, 128), BF16),
            pltpu.VMEM((8, ma, zd, slots, 128), BF16),
            pltpu.VMEM((kk * slots, 128), F32),
            pltpu.VMEM((M, M), BF16),
            pltpu.VMEM((2 * M, NPHI), BF16),
            pltpu.VMEM((NPHI, 2 * M), BF16),
            pltpu.VMEM((2 * M, NPHI), BF16),
            pltpu.VMEM((NPHI, 2 * M), BF16),
            pltpu.VMEM((NPHI, 256), BF16),
            pltpu.VMEM((4, ma, zd, slots, 128), BF16),
            pltpu.VMEM((4, ma, zd, slots, 128), BF16),
            pltpu.VMEM((4, nx, slots, kd, 128), BF16),
            pltpu.VMEM((4, nx, slots, kd, 128), BF16),
            pltpu.VMEM((slots, coef_rows, 128), F32),
            pltpu.VMEM((slots, coef_rows, 128), BF16),
            dma((2, slots)), dma((slots,)), dma((2,)), dma((slots,)),
            dma((8,)), dma((8,)), dma((4,)), dma((4,)),
            dma, dma, dma, dma,
            dma((8,)), dma((8,)), dma((4,)), dma((4,)),
        ],
        compiler_params=pltpu.CompilerParams(
            collective_id=1, has_side_effects=True, vmem_limit_bytes=60 * 2**20
        ),
    )(to_rows(forward_coef), to_rows(adjoint_coef), radial_table, jnp.asarray(fourier), jnp.asarray(fourier_t),
      jnp.asarray(cheb), jnp.asarray(cheb_t), radial_count, mode_blocks)
    blocks = rows.reshape(slots, kd * 2, nbs, 2, 128).transpose(0, 1, 3, 2, 4)
    return blocks.reshape(forward_coef.shape)


def solution(mesh):
    placed = (P("ma", "zg", None, None, None), P("ma", "zg", None, None, None), P("ma", None, None), P(), P())
    return jax.shard_map(
        functools.partial(body, MA_DIMS), mesh=mesh, in_specs=placed,
        out_specs=P("ma", "zg", None, None, None), check_vma=False,
    )
```

time: 139 us -> 119 us (0.86)
  matrix products: 14.9 us -> 0 us
  other arithmetic: 2.46 us -> 0 us
  local copies, waits for them, and re-layouts: 6.24 us -> 4.44 us
    dot_general x3 -> x0, matrix products: 14.9 us -> none  [the longest x2 9.21 us: body(): jnp.einsum('skcfn,snr->scfkr', coef, masked_table, preferred_element_type...]
    convert_element_type x1 -> x0, local copies, waits for them, and re-layouts: 3.49 us -> none  [body(): jnp.einsum('scgkr,snr->skcgn', back, masked_table, preferred_element_type...]
    unnamed x6 -> x1, local copies, waits for them, and re-layouts: 1.23 us -> 4.44 us
    add x2 -> x0, local copies, waits for them, and re-layouts: 1.52 us -> none  [body(): mode_blocks[:, None] * slots + slot_index[None, :]]
    mul x1 -> x0, other arithmetic: 1.44 us -> none  [body(): mode_blocks[:, None] * slots + slot_index[None, :]]
where the time goes in v1:
time: 119 us; the launch traced here: 118 us
  Pallas kernels  114 us (96%)
  local copies, waits for them, and re-layouts  4.44 us (4%)
    pallas_call x1, Pallas kernels, body(): pl.pallas_call(functools.partial(kernel, (nx, ma_dims, slots, kd, zd, nbs...  114 us
    unnamed x1, local copies, waits for them, and re-layouts  4.44 us

profile of v1, /device:TPU:0, one launch (start us, length us, event | category | flops | bytes accessed | tf_op | source)
XLA Modules:
  0.0 118.4 jit_solution(7978149814153548444)
XLA Ops:
  0.0 113.9 %shard_map.91 = bf16[16,512,128]{2,1,0:T(8,128)(2,1)} custom-call(bf16[16,512,128]{2,1,0:T(8,128)(2,1)} %bitcast.16, bf16[16,512,128]{2,1,0:T(8,128)(2,1)} %bitcast.17, bf16[16,512,512]{2,1,0:T(8,128)(2,1)} %radial_hbm.1, bf16[1024,1024]{1,0:T(8,128)(2,1)} %constant.8.clone.fourier_hbm, bf16[1024,1024]{1,0:T(8,128)(2,1)} %constant.9.clone.fourier_t_hbm, ...), custom_call_target="tpu_custom_call" | custom-call | tf_op jit(solution)/shard_map/pallas_call | solution.py:317
  113.9 4.4 %copy.14 = bf16[16,32,2,2,512]{4,3,2,1,0:T(2,128)(2,1)} copy(bf16[16,32,2,2,512]{4,3,2,1,0:T(2,128)(2,1)} %bitcast.15) | data formatting | bytes 4194304

commit v2 on v1

v2 whole, which is shorter than its diff:
```python
import functools
import math

import jax
import jax.numpy as jnp
import numpy as np
from jax import lax
from jax.experimental import pallas as pl
from jax.experimental.pallas import tpu as pltpu
from jax.sharding import PartitionSpec as P

M = 512
NN = 512
K = 128
NPHI = 1024
MA_DIMS = (4, 4, 2)
MESH = pl.DeviceIdType.MESH
BF16 = jnp.bfloat16
F32 = jnp.float32


def constant_tables():
    index = np.arange(M, dtype=np.int64)[:, None] * np.arange(NPHI, dtype=np.int64)[None, :] % NPHI
    angles = index.astype(np.float64) * (2.0 * math.pi / NPHI)
    fourier = np.concatenate([np.cos(angles), np.sin(angles)]) * math.sqrt(2.0 / NPHI)
    degree = np.arange(K, dtype=np.int64)
    cheb_index = degree[:, None] * (2 * degree[None, :] + 1) % (4 * K)
    cheb = np.cos(cheb_index.astype(np.float64) * (math.pi / (2 * K))) * math.sqrt(2.0 / K)
    fourier = fourier.astype(np.float32).astype(BF16)
    cheb = cheb.astype(np.float32).astype(BF16)
    return fourier, np.ascontiguousarray(fourier.T), cheb, np.ascontiguousarray(cheb.T)


def kernel(dims, coef0, coef1, radial_hbm, fourier_hbm, fourier_t_hbm, cheb_ref, cheb_t_ref, count_ref, block_ref,
           out_ref, coef, radial, wide, send_x, recv_x, send_y, recv_y, plane, one_hot, raw, raw_t, table, table_t,
           source, send_b, recv_b, send_o, recv_o,
           coef_sem, radial_sem, load_sem, local_x, local_y, local_b, local_o,
           ssem_x, ssem_y, ssem_b, ssem_o, sem_x, sem_y, sem_b, sem_o):
    nx, ma_dims, slots, kd, zd, nbs = dims
    ny, nz, nc = ma_dims
    ma = ny * nz * nc
    kk = nx * kd
    modes = ma * slots
    row_step = 4 * nbs
    x = lax.axis_index("zg")
    m = lax.axis_index("ma")
    my, mz, mc = m // (nz * nc), (m // nc) % nz, m % nc
    half = slots // 2
    x_order = (1,) if nx == 2 else tuple(range(2, nx - 1)) + (1, nx - 1)

    def far_first(i, n):
        return (2 + i + (i // 2) * (1 + 2 * (i % 2))) % 4 if n == 4 else n - 1 - i

    def ma_peer(j):
        dy, dz, dc = far_first(j // (nz * nc), ny), far_first((j // nc) % nz, nz), nc - 1 - j % nc
        return ((my + dy) % ny) * (nz * nc) + ((mz + dz) % nz) * nc + (mc + dc) % nc

    def x_peer(j):
        return (x + j) % nx

    def remote(src, dst, send_sem, recv_sem, to_x, to_m):
        return pltpu.make_async_remote_copy(
            src_ref=src, dst_ref=dst, send_sem=send_sem, recv_sem=recv_sem,
            device_id=(to_x, to_m), device_id_type=MESH,
        )

    def wait_received(buffer, ch, count, sem, local_sem):
        own = buffer.at[ch, 0]
        pltpu.make_async_copy(own, own, local_sem.at[ch]).wait()
        others = buffer.at[ch, pl.ds(0, count)]
        remote(others, others, sem.at[ch], sem.at[ch], x_peer(1), m).wait_recv()

    barrier = pltpu.get_barrier_semaphore()

    def signal_ma(j, carry):
        pl.semaphore_signal(barrier, inc=1, device_id=(x, ma_peer(j)), device_id_type=MESH)
        return carry

    lax.fori_loop(0, ma - 1, signal_ma, 0)
    for j in range(1, nx):
        pl.semaphore_signal(barrier, inc=1, device_id=(x_peer(j), m), device_id_type=MESH)

    def coef_load(arg, s):
        return pltpu.make_async_copy((coef0, coef1)[arg].at[s], coef.at[arg, s], coef_sem.at[arg, s])

    def radial_load(s):
        return pltpu.make_async_copy(radial_hbm.at[s], radial.at[s], radial_sem.at[s])

    def start_first(s, carry):
        coef_load(0, s).start()
        radial_load(s).start()
        return carry

    def start_second(s, carry):
        coef_load(1, s).start()
        return carry

    lax.fori_loop(0, slots, start_first, 0)
    lax.fori_loop(0, slots, start_second, 0)
    loads = [
        pltpu.make_async_copy(fourier_t_hbm, raw_t, load_sem.at[0]),
        pltpu.make_async_copy(fourier_hbm, raw, load_sem.at[1]),
    ]
    for load in loads:
        load.start()

    own_block = block_ref[m]
    lanes = lax.broadcasted_iota(jnp.int32, (1, 128), 1)
    low = lanes < 64

    def radial_slot(arg, s):
        coef_load(arg, s).wait()
        if arg == 0:
            radial_load(s).wait()
        live = count_ref[own_block * slots + s]
        wide[...] = coef[arg, s].astype(F32)
        rows = []
        for f in range(2):
            for part in range(2):
                tiles = []
                for nb in range(nbs):
                    tile = wide[pl.ds((part * nbs + nb) * 2 + f, kd, stride=row_step), :]
                    tiles.append(jnp.where(lanes + nb * 128 < live, tile, 0.0).astype(BF16))
                rows.append(jnp.concatenate(tiles, axis=1))
        values = jnp.dot(jnp.concatenate(rows, axis=0), radial[s], preferred_element_type=F32)
        for to in range(nx):
            first = values[:2 * kd, 128 * to:128 * (to + 1)]
            second = pltpu.roll(values[2 * kd:, 128 * to:128 * (to + 1)], 64, 1)
            halves = (jnp.where(low, first, second).astype(BF16), jnp.where(low, second, first).astype(BF16))
            for h in range(2):
                for part in range(2):
                    ch = ((h * 2 + arg) * 2 + s // half) * 2 + part
                    send_x[ch, to, s % half] = halves[h][part * kd:(part + 1) * kd]

    def x_send(ch):
        for j in x_order:
            remote(send_x.at[ch, x_peer(j)], recv_x.at[ch, x], ssem_x, sem_x.at[ch], x_peer(j), m).start()
        pltpu.make_async_copy(send_x.at[ch, x], recv_x.at[ch, x], local_x.at[ch]).start()

    def radial_first(s, carry):
        radial_slot(0, s)
        return carry

    def radial_second(s, carry):
        radial_slot(1, s)
        return carry

    lax.fori_loop(0, slots, radial_first, 0)
    pl.semaphore_wait(barrier, ma - 1 + nx - 1)
    for ch in range(4):
        x_send(ch)
    lax.fori_loop(0, slots, radial_second, 0)

    def one_hot_block(i, carry):
        part, pair = i // (ma // 2), i % (ma // 2)
        start = pl.multiple_of(i * 2 * half, 2 * half)
        column = lax.broadcasted_iota(jnp.int32, (2 * half, modes), 1)
        row = lax.broadcasted_iota(jnp.int32, (2 * half, modes), 0)
        first, second = block_ref[2 * pair] * slots, block_ref[2 * pair + 1] * slots
        mode = jnp.where(row < half, first + row, second + row - half) + part * half
        one_hot[pl.ds(start, 2 * half), :] = (column == mode).astype(F32).astype(BF16)
        return carry

    def make_tables():
        lax.fori_loop(0, ma, one_hot_block, 0)
        for load in loads:
            load.wait()
        for part in range(2):
            span = pl.ds(part * modes, modes)
            table_t[:, span] = lax.dot_general(
                raw_t[:, span], one_hot[...], (((1,), (1,)), ((), ())), preferred_element_type=F32).astype(BF16)
            table[span, :] = jnp.dot(one_hot[...], raw[span, :], preferred_element_type=F32).astype(BF16)

    def cheb_chunk(ahead, ch, carry):
        wait_received(recv_x, ch, nx - 1, sem_x, local_x)
        if ahead:
            x_send(ch + ahead)
        for s in range(0, half, 2):
            pair = jnp.concatenate([recv_x[ch, :, s + i].reshape(kk, 128) for i in range(2)], axis=1)
            levels = jnp.dot(cheb_t_ref[...], pair, preferred_element_type=F32)
            for i in range(2):
                plane[pl.ds(s + i, kk, stride=half), :] = levels[:, 128 * i:128 * (i + 1)]
        send_y[ch] = plane[...].astype(BF16).reshape(ma, zd // 2, 2 * half, 128)

        def send(j, carry):
            peer = ma_peer(j)
            remote(send_y.at[ch, peer], recv_y.at[ch, m], ssem_y, sem_y.at[ch], x, peer).start()
            return carry

        lax.fori_loop(0, ma - 1, send, 0)
        pltpu.make_async_copy(send_y.at[ch, m], recv_y.at[ch, m], local_y.at[ch]).start()
        return carry

    def wait_y(ch, carry):
        wait_received(recv_y, ch, ma - 1, sem_y, local_y)
        return carry

    def products(h, pair):
        columns = []
        for arg in range(2):
            levels = [[], []]
            for part in range(2):
                for sh in range(2):
                    tiles = recv_y[((h * 2 + arg) * 2 + sh) * 2 + part, :, pair].astype(F32)
                    tiles = tiles.reshape(ma, 2, half, 128)
                    for i in range(2):
                        levels[i].append(tiles[:, i].reshape(ma * half, 128).astype(BF16))
            columns.append([jnp.concatenate(level, axis=0) for level in levels])
        columns = [columns[arg][i] for i in range(2) for arg in range(2)]
        grid = jnp.dot(table_t[...], jnp.concatenate(columns, axis=1), preferred_element_type=F32)
        for i in range(2):
            forward = grid[:, 256 * i:256 * i + 128]
            adjoint = grid[:, 256 * i + 128:256 * i + 256]
            straight = forward * adjoint
            crossed = forward * pltpu.roll(adjoint, 64, 1)
            first = straight + pltpu.roll(straight, 64, 1)
            second = pltpu.roll(crossed, 64, 1) - crossed
            pick = (first, second) if h == 0 else (second, first)
            source[:, 128 * i:128 * (i + 1)] = jnp.where(low, pick[0], pick[1]).astype(BF16)
        back = jnp.dot(table[...], source[...], preferred_element_type=F32)
        for part in range(2):
            for sh in range(2):
                start = part * modes + sh * ma * half
                levels = [back[start:start + ma * half, 128 * i:128 * (i + 1)].reshape(ma, half, 128)
                          for i in range(2)]
                send_b[(h * 2 + sh) * 2 + part, :, pair] = jnp.concatenate(levels, axis=1).astype(BF16)

    def back_send(ch):
        def send(j, carry):
            peer = ma_peer(j)
            remote(send_b.at[ch, peer], recv_b.at[ch, m], ssem_b, sem_b.at[ch], x, peer).start()
            return carry

        lax.fori_loop(0, ma - 1, send, 0)
        pltpu.make_async_copy(send_b.at[ch, m], recv_b.at[ch, m], local_b.at[ch]).start()

    ahead_chunk = functools.partial(cheb_chunk, 4)
    last_chunk = functools.partial(cheb_chunk, 0)
    lax.fori_loop(0, 4, ahead_chunk, 0)
    make_tables()
    lax.fori_loop(4, 11, ahead_chunk, 0)
    lax.fori_loop(0, 8, wait_y, 0)
    for pair in range(zd // 2):
        products(0, pair)
        if pair == 0:
            lax.fori_loop(11, 12, ahead_chunk, 0)
    lax.fori_loop(12, 16, last_chunk, 0)

    def drain(i, carry):
        back_send(i)
        wait_y(8 + 2 * i, 0)
        wait_y(9 + 2 * i, 0)
        return carry

    lax.fori_loop(0, 4, drain, 0)
    def cheb_back(more, groups, ch, carry):
        wait_received(recv_b, ch, ma - 1, sem_b, local_b)
        if more:
            back_send(ch + more)
        plane[...] = recv_b[ch].reshape(kk * half, 128).astype(F32)
        size = half // groups
        for group in range(groups):
            for s in range(group * size, (group + 1) * size, 2):
                pair = jnp.concatenate(
                    [plane[pl.ds(s + i, kk, stride=half), :] for i in range(2)], axis=1).astype(BF16)
                degrees = jnp.dot(cheb_ref[...], pair, preferred_element_type=F32).astype(BF16)
                for i in range(2):
                    send_o[ch, :, s + i] = degrees[:, 128 * i:128 * (i + 1)].reshape(nx, kd, 128)
            span = pl.ds(group * size, size)
            for j in x_order:
                remote(send_o.at[ch, x_peer(j), span], recv_o.at[ch, x, span],
                       ssem_o, sem_o.at[ch, group], x_peer(j), m).start()
        pltpu.make_async_copy(send_o.at[ch, x], recv_o.at[ch, x], local_o.at[ch]).start()
        return carry

    for pair in range(zd // 2):
        products(1, pair)
        if pair == 0:
            lax.fori_loop(0, 1, functools.partial(cheb_back, 0, 1), 0)
    back_send(4)
    back_send(5)
    lax.fori_loop(1, 3, functools.partial(cheb_back, 5, 1), 0)
    lax.fori_loop(3, 6, functools.partial(cheb_back, 0, 1), 0)
    lax.fori_loop(6, 8, functools.partial(cheb_back, 0, half // 2), 0)

    def radial_back(s, carry):
        sh = s // half
        live = count_ref[own_block * slots + s]
        rows = []
        for part in range(2):
            first, second = [], []
            for at in range(nx):
                near = recv_o[sh * 2 + part, at, s % half].astype(F32)
                far = recv_o[4 + sh * 2 + part, at, s % half].astype(F32)
                first.append(jnp.where(low, near, far).astype(BF16))
                second.append(pltpu.roll(jnp.where(low, far, near), 64, 1).astype(BF16))
            rows += [jnp.concatenate(first, axis=1), jnp.concatenate(second, axis=1)]
        values = lax.dot_general(
            jnp.concatenate(rows, axis=0), radial[s], (((1,), (1,)), ((), ())), preferred_element_type=F32)
        for part in range(2):
            for g in range(2):
                for nb in range(nbs):
                    tile = values[(part * 2 + g) * kd:(part * 2 + g + 1) * kd, 128 * nb:128 * (nb + 1)]
                    wide[pl.ds((part * nbs + nb) * 2 + g, kd, stride=row_step), :] = jnp.where(
                        lanes + nb * 128 < live, tile, 0.0)
        out_ref[s] = wide[...].astype(BF16)
        return carry

    def wait_o(ch, groups):
        own = recv_o.at[ch, x]
        pltpu.make_async_copy(own, own, local_o.at[ch]).wait()
        if groups == 1:
            wait_group(ch, 0, half)

    def wait_group(ch, group, size):
        others = recv_o.at[ch, pl.ds(0, nx - 1), pl.ds(group * size, size)]
        remote(others, others, sem_o.at[ch, group], sem_o.at[ch, group], x_peer(1), m).wait_recv()

    for ch in (0, 1, 4, 5):
        wait_o(ch, 1)
    lax.fori_loop(0, half, radial_back, 0)
    for ch in (2, 3):
        wait_o(ch, 1)
    for ch in (6, 7):
        wait_o(ch, half // 2)

    def last_slots(group, carry):
        for ch in (6, 7):
            wait_group(ch, group, 2)
        return lax.fori_loop(half + 2 * group, half + 2 * group + 2, radial_back, carry)

    lax.fori_loop(0, half // 2, last_slots, 0)

    for buffer, count, sem in (
        (recv_x, nx - 1, ssem_x), (recv_y, ma - 1, ssem_y), (recv_b, ma - 1, ssem_b), (recv_o, nx - 1, ssem_o)
    ):
        sent = buffer.at[:, pl.ds(0, count)]
        remote(sent, sent, sem, sem, x_peer(1), m).wait_send()


def body(ma_dims, forward_coef, adjoint_coef, radial_table, radial_count, mode_blocks):
    nx = lax.axis_size("zg")
    ma = lax.axis_size("ma")
    slots, kd = forward_coef.shape[:2]
    kk = nx * kd
    zd = kk // ma
    nbs = NN // 128
    coef_rows = kd * 2 * nbs * 2

    def to_rows(array):
        blocks = array.reshape(slots, kd * 2, 2, nbs, 128).transpose(0, 1, 3, 2, 4)
        return blocks.reshape(slots, coef_rows, 128)

    fourier, fourier_t, cheb, cheb_t = constant_tables()
    any_spec = pl.BlockSpec(memory_space=pl.ANY)
    vmem_spec = pl.BlockSpec(memory_space=pltpu.VMEM)
    smem_spec = pl.BlockSpec(memory_space=pltpu.SMEM)
    dma = pltpu.SemaphoreType.DMA
    rows = pl.pallas_call(
        functools.partial(kernel, (nx, ma_dims, slots, kd, zd, nbs)),
        out_shape=pltpu.VMEM((slots, coef_rows, 128), BF16),
        in_specs=[any_spec] * 5 + [vmem_spec] * 2 + [smem_spec] * 2,
        out_specs=vmem_spec,
        scratch_shapes=[
            pltpu.VMEM((2, slots, coef_rows, 128), BF16),
            pltpu.VMEM(radial_table.shape, BF16),
            pltpu.VMEM((coef_rows, 128), F32),
            pltpu.VMEM((16, nx, slots // 2, kd, 128), BF16),
            pltpu.VMEM((16, nx, slots // 2, kd, 128), BF16),
            pltpu.VMEM((16, ma, zd // 2, slots, 128), BF16),
            pltpu.VMEM((16, ma, zd // 2, slots, 128), BF16),
            pltpu.VMEM((kk * slots // 2, 128), F32),
            pltpu.VMEM((M, M), BF16),
            pltpu.VMEM((2 * M, NPHI), BF16),
            pltpu.VMEM((NPHI, 2 * M), BF16),
            pltpu.VMEM((2 * M, NPHI), BF16),
            pltpu.VMEM((NPHI, 2 * M), BF16),
            pltpu.VMEM((NPHI, 256), BF16),
            pltpu.VMEM((8, ma, zd // 2, slots, 128), BF16),
            pltpu.VMEM((8, ma, zd // 2, slots, 128), BF16),
            pltpu.VMEM((8, nx, slots // 2, kd, 128), BF16),
            pltpu.VMEM((8, nx, slots // 2, kd, 128), BF16),
            dma((2, slots)), dma((slots,)), dma((2,)),
            dma((16,)), dma((16,)), dma((8,)), dma((8,)),
            dma, dma, dma, dma,
            dma((16,)), dma((16,)), dma((8,)), dma((8, slots // 4)),
        ],
        compiler_params=pltpu.CompilerParams(
            collective_id=1, has_side_effects=True, vmem_limit_bytes=60 * 2**20
        ),
    )(to_rows(forward_coef), to_rows(adjoint_coef), radial_table, jnp.asarray(fourier), jnp.asarray(fourier_t),
      jnp.asarray(cheb), jnp.asarray(cheb_t), radial_count, mode_blocks)
    blocks = rows.reshape(slots, kd * 2, nbs, 2, 128).transpose(0, 1, 3, 2, 4)
    return blocks.reshape(forward_coef.shape)


def solution(mesh):
    placed = (P("ma", "zg", None, None, None), P("ma", "zg", None, None, None), P("ma", None, None), P(), P())
    return jax.shard_map(
        functools.partial(body, MA_DIMS), mesh=mesh, in_specs=placed,
        out_specs=P("ma", "zg", None, None, None), check_vma=False,
    )
```

time: 119 us -> 110 us (0.924)
  Pallas kernels: 114 us -> 108 us
  local copies, waits for them, and re-layouts: 4.44 us -> 1.32 us
    pallas_call x1, Pallas kernels: 114 us -> 108 us  [body(): pl.pallas_call(functools.partial(kernel, (nx, ma_dims, slots, kd, zd, nbs...]
    unnamed x1, local copies, waits for them, and re-layouts: 4.44 us -> 1.32 us
where the time goes in v2:
time: 110 us
  Pallas kernels  108 us (98%)
  local copies, waits for them, and re-layouts  1.32 us (1%)
    pallas_call x1, Pallas kernels, body(): pl.pallas_call(functools.partial(kernel, (nx, ma_dims, slots, kd, zd, nbs...  108 us

profile of v2, /device:TPU:0, one launch (start us, length us, event | category | flops | bytes accessed | tf_op | source)
XLA Modules:
  0.0 109.5 jit_solution(6458477747680727749)
XLA Ops:
  0.0 108.2 %shard_map.91 = bf16[16,512,128]{2,1,0:T(8,128)(2,1)S(1)} custom-call(bf16[16,512,128]{2,1,0:T(8,128)(2,1)} %bitcast.16, bf16[16,512,128]{2,1,0:T(8,128)(2,1)} %bitcast.17, bf16[16,512,512]{2,1,0:T(8,128)(2,1)} %radial_hbm.1, bf16[1024,1024]{1,0:T(8,128)(2,1)} %constant.8.clone.fourier_hbm, bf16[1024,1024]{1,0:T(8,128)(2,1)} %constant.9.clone.fourier_t_hbm, ...), custom_call_target="tpu_custom_call" | custom-call | tf_op jit(solution)/shard_map/pallas_call | solution.py:359
  108.2 1.3 %copy.14 = bf16[16,32,2,2,512]{4,3,2,1,0:T(2,128)(2,1)} copy(bf16[16,32,2,2,512]{4,3,2,1,0:T(2,128)(2,1)S(1)} %bitcast.15) | data formatting | bytes 4194304

commit v3 on v2

--- a/solution.py
+++ b/solution.py
@@ -58,6 +58,8 @@
     def x_peer(j):
         return (x + j) % nx
 
+    peers = [ma_peer(j) for j in range(ma - 1)]
+
     def remote(src, dst, send_sem, recv_sem, to_x, to_m):
         return pltpu.make_async_remote_copy(
             src_ref=src, dst_ref=dst, send_sem=send_sem, recv_sem=recv_sem,
@@ -72,11 +74,8 @@
 
     barrier = pltpu.get_barrier_semaphore()
 
-    def signal_ma(j, carry):
-        pl.semaphore_signal(barrier, inc=1, device_id=(x, ma_peer(j)), device_id_type=MESH)
-        return carry
-
-    lax.fori_loop(0, ma - 1, signal_ma, 0)
+    for peer in peers:
+        pl.semaphore_signal(barrier, inc=1, device_id=(x, peer), device_id_type=MESH)
     for j in range(1, nx):
         pl.semaphore_signal(barrier, inc=1, device_id=(x_peer(j), m), device_id_type=MESH)
 
@@ -86,17 +85,11 @@
     def radial_load(s):
         return pltpu.make_async_copy(radial_hbm.at[s], radial.at[s], radial_sem.at[s])
 
-    def start_first(s, carry):
+    for s in range(slots):
         coef_load(0, s).start()
         radial_load(s).start()
-        return carry
-
-    def start_second(s, carry):
+    for s in range(slots):
         coef_load(1, s).start()
-        return carry
-
-    lax.fori_loop(0, slots, start_first, 0)
-    lax.fori_loop(0, slots, start_second, 0)
     loads = [
         pltpu.make_async_copy(fourier_t_hbm, raw_t, load_sem.at[0]),
         pltpu.make_async_copy(fourier_hbm, raw, load_sem.at[1]),
@@ -182,12 +175,8 @@
                 plane[pl.ds(s + i, kk, stride=half), :] = levels[:, 128 * i:128 * (i + 1)]
         send_y[ch] = plane[...].astype(BF16).reshape(ma, zd // 2, 2 * half, 128)
 
-        def send(j, carry):
-            peer = ma_peer(j)
+        for peer in peers:
             remote(send_y.at[ch, peer], recv_y.at[ch, m], ssem_y, sem_y.at[ch], x, peer).start()
-            return carry
-
-        lax.fori_loop(0, ma - 1, send, 0)
         pltpu.make_async_copy(send_y.at[ch, m], recv_y.at[ch, m], local_y.at[ch]).start()
         return carry
 
@@ -226,12 +215,8 @@
                 send_b[(h * 2 + sh) * 2 + part, :, pair] = jnp.concatenate(levels, axis=1).astype(BF16)
 
     def back_send(ch):
-        def send(j, carry):
-            peer = ma_peer(j)
+        for peer in peers:
             remote(send_b.at[ch, peer], recv_b.at[ch, m], ssem_b, sem_b.at[ch], x, peer).start()
-            return carry
-
-        lax.fori_loop(0, ma - 1, send, 0)
         pltpu.make_async_copy(send_b.at[ch, m], recv_b.at[ch, m], local_b.at[ch]).start()
 
     ahead_chunk = functools.partial(cheb_chunk, 4)
@@ -277,8 +262,8 @@
         products(1, pair)
         if pair == 0:
             lax.fori_loop(0, 1, functools.partial(cheb_back, 0, 1), 0)
-    back_send(4)
-    back_send(5)
+    for ch in (4, 5):
+        back_send(ch)
     lax.fori_loop(1, 3, functools.partial(cheb_back, 5, 1), 0)
     lax.fori_loop(3, 6, functools.partial(cheb_back, 0, 1), 0)
     lax.fori_loop(6, 8, functools.partial(cheb_back, 0, half // 2), 0)

time: 110 us -> 102 us (0.927)
  Pallas kernels: 108 us -> 101 us
    pallas_call x1, Pallas kernels: 108 us -> 101 us  [body(): pl.pallas_call(functools.partial(kernel, (nx, ma_dims, slots, kd, zd, nbs...]
where the time goes in v3:
time: 102 us
  Pallas kernels  101 us (99%)
  local copies, waits for them, and re-layouts  1.32 us (1%)
    pallas_call x1, Pallas kernels, body(): pl.pallas_call(functools.partial(kernel, (nx, ma_dims, slots, kd, zd, nbs...  101 us

profile of v3, /device:TPU:0, one launch (start us, length us, event | category | flops | bytes accessed | tf_op | source)
XLA Modules:
  0.0 101.9 jit_solution(16382254098749941867)
XLA Ops:
  0.0 100.6 %shard_map.91 = bf16[16,512,128]{2,1,0:T(8,128)(2,1)S(1)} custom-call(bf16[16,512,128]{2,1,0:T(8,128)(2,1)} %bitcast.16, bf16[16,512,128]{2,1,0:T(8,128)(2,1)} %bitcast.17, bf16[16,512,512]{2,1,0:T(8,128)(2,1)} %radial_hbm.1, bf16[1024,1024]{1,0:T(8,128)(2,1)} %constant.8.clone.fourier_hbm, bf16[1024,1024]{1,0:T(8,128)(2,1)} %constant.9.clone.fourier_t_hbm, ...), custom_call_target="tpu_custom_call" | custom-call | tf_op jit(solution)/shard_map/pallas_call | solution.py:344
  100.6 1.3 %copy.14 = bf16[16,32,2,2,512]{4,3,2,1,0:T(2,128)(2,1)} copy(bf16[16,32,2,2,512]{4,3,2,1,0:T(2,128)(2,1)S(1)} %bitcast.15) | data formatting | bytes 4194304

commit v4 on v3

--- a/solution.py
+++ b/solution.py
@@ -33,7 +33,7 @@
 
 def kernel(dims, coef0, coef1, radial_hbm, fourier_hbm, fourier_t_hbm, cheb_ref, cheb_t_ref, count_ref, block_ref,
            out_ref, coef, radial, wide, send_x, recv_x, send_y, recv_y, plane, one_hot, raw, raw_t, table, table_t,
-           source, send_b, recv_b, send_o, recv_o,
+           grid0, source, send_b, recv_b, send_o, recv_o,
            coef_sem, radial_sem, load_sem, local_x, local_y, local_b, local_o,
            ssem_x, ssem_y, ssem_b, ssem_o, sem_x, sem_y, sem_b, sem_o):
     nx, ma_dims, slots, kd, zd, nbs = dims
@@ -184,22 +184,26 @@
         wait_received(recv_y, ch, ma - 1, sem_y, local_y)
         return carry
 
+    def synthesis(h, arg, pair):
+        levels = [[], []]
+        for part in range(2):
+            for sh in range(2):
+                tiles = recv_y[((h * 2 + arg) * 2 + sh) * 2 + part, :, pair].astype(F32)
+                tiles = tiles.reshape(ma, 2, half, 128)
+                for i in range(2):
+                    levels[i].append(tiles[:, i].reshape(ma * half, 128).astype(BF16))
+        columns = jnp.concatenate([jnp.concatenate(level, axis=0) for level in levels], axis=1)
+        return jnp.dot(table_t[...], columns, preferred_element_type=F32)
+
+    def forward_grids(h):
+        for pair in range(zd // 2):
+            grid0[pair] = synthesis(h, 0, pair)
+
     def products(h, pair):
-        columns = []
-        for arg in range(2):
-            levels = [[], []]
-            for part in range(2):
-                for sh in range(2):
-                    tiles = recv_y[((h * 2 + arg) * 2 + sh) * 2 + part, :, pair].astype(F32)
-                    tiles = tiles.reshape(ma, 2, half, 128)
-                    for i in range(2):
-                        levels[i].append(tiles[:, i].reshape(ma * half, 128).astype(BF16))
-            columns.append([jnp.concatenate(level, axis=0) for level in levels])
-        columns = [columns[arg][i] for i in range(2) for arg in range(2)]
-        grid = jnp.dot(table_t[...], jnp.concatenate(columns, axis=1), preferred_element_type=F32)
+        grid = synthesis(h, 1, pair)
         for i in range(2):
-            forward = grid[:, 256 * i:256 * i + 128]
-            adjoint = grid[:, 256 * i + 128:256 * i + 256]
+            forward = grid0[pair, :, 128 * i:128 * (i + 1)]
+            adjoint = grid[:, 128 * i:128 * (i + 1)]
             straight = forward * adjoint
             crossed = forward * pltpu.roll(adjoint, 64, 1)
             first = straight + pltpu.roll(straight, 64, 1)
@@ -223,18 +227,23 @@
     last_chunk = functools.partial(cheb_chunk, 0)
     lax.fori_loop(0, 4, ahead_chunk, 0)
     make_tables()
-    lax.fori_loop(4, 11, ahead_chunk, 0)
-    lax.fori_loop(0, 8, wait_y, 0)
+    lax.fori_loop(4, 8, ahead_chunk, 0)
+    lax.fori_loop(0, 4, wait_y, 0)
+    forward_grids(0)
+    lax.fori_loop(8, 11, ahead_chunk, 0)
+    lax.fori_loop(4, 8, wait_y, 0)
     for pair in range(zd // 2):
         products(0, pair)
         if pair == 0:
             lax.fori_loop(11, 12, ahead_chunk, 0)
-    lax.fori_loop(12, 16, last_chunk, 0)
+    lax.fori_loop(12, 15, last_chunk, 0)
+    lax.fori_loop(8, 12, wait_y, 0)
+    forward_grids(1)
+    lax.fori_loop(15, 16, last_chunk, 0)
 
     def drain(i, carry):
         back_send(i)
-        wait_y(8 + 2 * i, 0)
-        wait_y(9 + 2 * i, 0)
+        wait_y(12 + i, 0)
         return carry
 
     lax.fori_loop(0, 4, drain, 0)
@@ -360,6 +369,7 @@
             pltpu.VMEM((NPHI, 2 * M), BF16),
             pltpu.VMEM((2 * M, NPHI), BF16),
             pltpu.VMEM((NPHI, 2 * M), BF16),
+            pltpu.VMEM((zd // 2, NPHI, 256), F32),
             pltpu.VMEM((NPHI, 256), BF16),
             pltpu.VMEM((8, ma, zd // 2, slots, 128), BF16),
             pltpu.VMEM((8, ma, zd // 2, slots, 128), BF16),

time: 102 us -> 102 us (level)
  no operation moved by 1% of the time
where the time goes in v4:
time: 102 us
  Pallas kernels  101 us (99%)
  local copies, waits for them, and re-layouts  1.32 us (1%)
    pallas_call x1, Pallas kernels, body(): pl.pallas_call(functools.partial(kernel, (nx, ma_dims, slots, kd, zd, nbs...  101 us

profile of v4, /device:TPU:0, one launch (start us, length us, event | category | flops | bytes accessed | tf_op | source)
XLA Modules:
  0.0 101.9 jit_solution(17275351767120535988)
XLA Ops:
  0.0 100.5 %shard_map.91 = bf16[16,512,128]{2,1,0:T(8,128)(2,1)S(1)} custom-call(bf16[16,512,128]{2,1,0:T(8,128)(2,1)} %bitcast.16, bf16[16,512,128]{2,1,0:T(8,128)(2,1)} %bitcast.17, bf16[16,512,512]{2,1,0:T(8,128)(2,1)} %radial_hbm.1, bf16[1024,1024]{1,0:T(8,128)(2,1)} %constant.8.clone.fourier_hbm, bf16[1024,1024]{1,0:T(8,128)(2,1)} %constant.9.clone.fourier_t_hbm, ...), custom_call_target="tpu_custom_call" | custom-call | tf_op jit(solution)/shard_map/pallas_call | solution.py:353
  100.6 1.3 %copy.14 = bf16[16,32,2,2,512]{4,3,2,1,0:T(2,128)(2,1)} copy(bf16[16,32,2,2,512]{4,3,2,1,0:T(2,128)(2,1)S(1)} %bitcast.15) | data formatting | bytes 4194304

commit v5 on v4

--- a/solution.py
+++ b/solution.py
@@ -277,7 +277,7 @@
     lax.fori_loop(3, 6, functools.partial(cheb_back, 0, 1), 0)
     lax.fori_loop(6, 8, functools.partial(cheb_back, 0, half // 2), 0)
 
-    def radial_back(s, carry):
+    def radial_back(s, base):
         sh = s // half
         live = count_ref[own_block * slots + s]
         rows = []
@@ -295,9 +295,13 @@
             for g in range(2):
                 for nb in range(nbs):
                     tile = values[(part * 2 + g) * kd:(part * 2 + g + 1) * kd, 128 * nb:128 * (nb + 1)]
-                    wide[pl.ds((part * nbs + nb) * 2 + g, kd, stride=row_step), :] = jnp.where(
+                    plane[pl.ds(base + (part * nbs + nb) * 2 + g, kd, stride=row_step), :] = jnp.where(
                         lanes + nb * 128 < live, tile, 0.0)
-        out_ref[s] = wide[...].astype(BF16)
+        out_ref[s] = plane[pl.ds(base, 2 * nbs * 2 * kd), :].astype(BF16)
+
+    def radial_pair(i, carry):
+        for k in range(2):
+            radial_back(2 * i + k, k * 2 * nbs * 2 * kd)
         return carry
 
     def wait_o(ch, groups):
@@ -312,7 +316,7 @@
 
     for ch in (0, 1, 4, 5):
         wait_o(ch, 1)
-    lax.fori_loop(0, half, radial_back, 0)
+    lax.fori_loop(0, half // 2, radial_pair, 0)
     for ch in (2, 3):
         wait_o(ch, 1)
     for ch in (6, 7):
@@ -321,7 +325,7 @@
     def last_slots(group, carry):
         for ch in (6, 7):
             wait_group(ch, group, 2)
-        return lax.fori_loop(half + 2 * group, half + 2 * group + 2, radial_back, carry)
+        return radial_pair(half // 2 + group, carry)
 
     lax.fori_loop(0, half // 2, last_slots, 0)
 

time: 102 us -> 102 us (level)
  no operation moved by 1% of the time
where the time goes in v5:
time: 102 us; the launch traced here: 101 us
  Pallas kernels  100 us (98%)
  local copies, waits for them, and re-layouts  1.32 us (1%)
    pallas_call x1, Pallas kernels, body(): pl.pallas_call(functools.partial(kernel, (nx, ma_dims, slots, kd, zd, nbs...  100 us

profile of v5, /device:TPU:0, one launch (start us, length us, event | category | flops | bytes accessed | tf_op | source)
XLA Modules:
  0.0 101.4 jit_solution(10243944341900695603)
XLA Ops:
  0.0 100.0 %shard_map.91 = bf16[16,512,128]{2,1,0:T(8,128)(2,1)S(1)} custom-call(bf16[16,512,128]{2,1,0:T(8,128)(2,1)} %bitcast.16, bf16[16,512,128]{2,1,0:T(8,128)(2,1)} %bitcast.17, bf16[16,512,512]{2,1,0:T(8,128)(2,1)} %radial_hbm.1, bf16[1024,1024]{1,0:T(8,128)(2,1)} %constant.8.clone.fourier_hbm, bf16[1024,1024]{1,0:T(8,128)(2,1)} %constant.9.clone.fourier_t_hbm, ...), custom_call_target="tpu_custom_call" | custom-call | tf_op jit(solution)/shard_map/pallas_call | solution.py:357
  100.1 1.3 %copy.14 = bf16[16,32,2,2,512]{4,3,2,1,0:T(2,128)(2,1)} copy(bf16[16,32,2,2,512]{4,3,2,1,0:T(2,128)(2,1)S(1)} %bitcast.15) | data formatting | bytes 4194304
